TPU v7x, 256 devices: a whole 4x4x8 slice. The times are simulated.
256 devices in a mesh: dp: 16 (over z_lo, y, core), tensor: 16 (over z_hi, x).
Axes of the slice: x: 4, y: 4, z: 8 (z_hi: 4, z_lo: 2; z = z_hi * 2 + z_lo), core: 2. Of those that a mesh axis runs over, the one named last changes fastest.
Arguments:
- tokens: bfloat16 [131072, 3072], P(('dp', 'tensor')), parts along dimension 0, may hold values from -6 to 6
- expert_ids: int32 [131072, 4], P(('dp', 'tensor')), parts along dimension 0, may hold values from 0 to 15, as said below
- gate_probs: float32 [131072, 4], P(('dp', 'tensor')), parts along dimension 0, may hold values from 0.1 to 1
- gate_weight: bfloat16 [3072, 5376], P(None, 'tensor'), may hold values from -0.109375 to 0.109375
- up_weight: bfloat16 [3072, 5376], P(None, 'tensor'), may hold values from -0.109375 to 0.109375
- down_weight: bfloat16 [5376, 3072], P('tensor'), may hold values from -0.078125 to 0.078125
Outputs:
- mixed: bfloat16 [131072, 3072], P(('dp', 'tensor')), parts along dimension 0
There are 16 independent parts, one for each index of `dp`. A program takes and returns all parts, laid end to end along the dimension named above; an argument that names none is the same for every part. Nothing has to cross between parts.
Inputs may be any that keep to these rules, and one draw needn't show every extreme that they name: `expert_ids`: each row names 4 different experts. In each block of 128 consecutive tokens (rows b * 128 to (b + 1) * 128 - 1) between 1 and 32 rows name expert 0, and some block has exactly 32.
All inputs are finite; a program needn't handle non-finite values.
Results may differ from a plain program's by a relative error of at most 0.019.
Values may be sent and summed in bfloat16 or wider, within the bound.
No kernel may reach another device: no remote copies, remote signals or barrier semaphores. Data moves between devices by JAX's collectives and lax.ppermute only.
A program may use at most 128 MiB of HBM per device.

v0:
```python
import jax
import jax.numpy as jnp
from jax import lax
from jax.sharding import PartitionSpec as P

SPANS = 4
CT = 128
CAP = 32


def on_device(tokens, expert_ids, gate_probs, gate_weight, up_weight, down_weight):
    model_width = tokens.shape[1]
    is_window = expert_ids == 0
    routed = jnp.any(is_window, axis=1)
    gate_share = jnp.sum(jnp.where(is_window, gate_probs, 0.0), axis=1)
    routed_blocks = routed.reshape(SPANS, CT)
    slot_place = jnp.cumsum(routed_blocks.astype(jnp.int32), axis=1) - 1
    selector = (
        slot_place[:, None, :] == jnp.arange(CAP, dtype=jnp.int32)[None, :, None]
    ) & routed_blocks[:, None, :]
    slot_rows = jnp.einsum(
        "bst,btd->bsd",
        selector.astype(jnp.bfloat16),
        tokens.reshape(SPANS, CT, model_width),
        preferred_element_type=jnp.float32,
    ).astype(jnp.bfloat16)
    row_piece = lax.all_gather(
        slot_rows.reshape(SPANS * CAP, model_width), "tensor", axis=0, tiled=True
    )
    gate_pre = jnp.dot(row_piece, gate_weight, preferred_element_type=jnp.float32)
    up_pre = jnp.dot(row_piece, up_weight, preferred_element_type=jnp.float32)
    hidden = (jax.nn.silu(gate_pre) * up_pre).astype(jnp.bfloat16)
    partial_rows = jnp.dot(hidden, down_weight, preferred_element_type=jnp.float32)
    expert_out = lax.psum_scatter(
        partial_rows.astype(jnp.bfloat16), "tensor", scatter_dimension=0, tiled=True
    ).astype(jnp.float32)
    slot_index = jnp.where(
        routed_blocks, jnp.arange(SPANS, dtype=jnp.int32)[:, None] * CAP + slot_place, 0
    )
    picked = jnp.take(expert_out, slot_index.reshape(-1), axis=0)
    mixed = jnp.where(routed[:, None], gate_share[:, None] * picked, 0.0)
    return mixed.astype(jnp.bfloat16)


def solution(mesh):
    in_specs = (
        P(("dp", "tensor"), None),
        P(("dp", "tensor"), None),
        P(("dp", "tensor"), None),
        P(None, "tensor"),
        P(None, "tensor"),
        P("tensor", None),
    )
    out_specs = P(("dp", "tensor"), None)
    return jax.shard_map(
        on_device, mesh=mesh, in_specs=in_specs, out_specs=out_specs, check_vma=False
    )
```

profile of v0, /device:TPU:1, one launch (start us, length us, event | category | flops | bytes accessed | tf_op | source)
XLA Modules:
  0.0 385.3 jit_solution(9440942069430270714)
XLA Ops:
  6.5 0.0 copy-start
  6.5 0.0 all-gather.2.cloned.1.call-start
  6.5 0.9 select_reduce_fusion
  7.5 0.3 reduce_window_sum.11
  7.8 0.7 copy-done
  8.5 1.4 convolution_convert_fusion.1
  9.9 0.0 all-gather.2.cloned.1.call-update
  9.9 0.0 reduce-scatter.2.cloned.1.call-start
  10.0 160.2 %all-gather.2.cloned.1.call-done = bf16[2048,3072]{1,0:T(8,128)(2,1)} async-done(((bf16[128,3072]{1,0:T(8,128)(2,1)}), bf16[2048,3072]{1,0:T(8,128)(2,1)}) %all-gather.2.cloned.1.call-update) | async-done | bytes 12582928 | tf_op jit(solution)/shard_map/all_gather | solution.py:27
  170.1 11.1 %fusion.7 = f32[2048,336]{0,1:T(8,128)} fusion(bf16[2048,3072]{1,0:T(8,128)(2,1)} %all-gather.2.cloned.1.call-done, bf16[3072,336]{0,1:T(8,128)(2,1)} %param.9), kind=kOutput, calls=%fused_computation.24 | convolution fusion | flops 4227858432 | bytes 17399808 | tf_op jit(solution)/shard_map/dot_general | solution.py:30
  181.3 18.5 %convolution_convert_fusion = bf16[2048,3072]{1,0:T(8,128)(2,1)} fusion(bf16[336,3072]{1,0:T(8,128)(2,1)} %param.11, bf16[2048,3072]{1,0:T(8,128)(2,1)} %all-gather.2.cloned.1.call-done, bf16[3072,336]{0,1:T(8,128)(2,1)} %param.10, f32[2048,336]{0,1:T(8,128)} %fusion.7), kind=kOutput, calls=%fused_computation.1 | convolution fusion | flops 8466137088 | bytes 32047104 | tf_op jit(solution)/shard_map/dot_general | solution.py:33
  199.8 0.0 reduce-scatter.2.cloned.1.call-update
  199.8 0.1 compare_and_fusion
  199.9 162.5 %reduce-scatter.2.cloned.1.call-done = bf16[128,3072]{1,0:T(8,128)(2,1)} async-done(((bf16[2048,3072]{1,0:T(8,128)(2,1)}), bf16[128,3072]{1,0:T(8,128)(2,1)}) %reduce-scatter.2.cloned.1.call-update) | async-done | bytes 786448 | tf_op jit(solution)/shard_map/reduce_scatter | solution.py:34
  362.4 2.4 convert_element_type.23
  364.9 8.7 %gather_fusion = f32[512,3072]{1,0:T(8,128)} fusion(f32[128,3072]{1,0:T(8,128)} %convert_element_type.23, s32[1024]{0:T(1024)S(1)} %pad_clamp_fusion), kind=kCustom, calls=%fused_computation | custom fusion | bytes 12584960 | tf_op jit(solution)/shard_map/jit(_take)/gather | solution.py:40
  373.6 4.9 %select_convert_fusion = bf16[512,3072]{1,0:T(8,128)(2,1)} fusion(f32[512,3072]{1,0:T(8,128)} %gather_fusion, f32[512]{0:T(512)S(1)} %get-tuple-element.7, pred[512]{0:T(512)(128)(4,1)S(1)} %get-tuple-element.5, pred[512]{0:T(512)(128)(4,1)S(1)} %reduce_or.11), kind=kLoop, calls=%fused_computation.2 | loop fusion | flops 6291456 | bytes 9440256 | tf_op jit(solution)/shard_map/convert_element_type | solution.py:42
  (6 shorter events, 0.1 us)
Async XLA Ops:
  6.5 1.9 copy-start
  6.5 163.6 %all-gather.2.cloned.1.call-start = ((), (), s32[]{:S(2)}) async-start(), calls=%async_computation.1 | async-start | bytes 13369344 | tf_op jit(solution)/shard_map/all_gather | solution.py:27
  9.9 352.5 %reduce-scatter.2.cloned.1.call-start = ((), (), s32[]{:S(2)}) async-start(), calls=%async_computation.2 | async-start | bytes 13369344 | tf_op jit(solution)/shard_map/reduce_scatter | solution.py:34
Sparse Core Ops, SparseCore 0:
  10.0 160.0 all-gather.1
  199.9 162.4 reduce-scatter.1
where the time goes:
time: 385 us
  waiting for transfers between devices  323 us (84%)
  matrix products  31.1 us (8%)
  between operations  13.4 us (3%)
  local copies, waits for them, and re-layouts  9.41 us (2%)
  other arithmetic  8.61 us (2%)
    reduce_scatter x1, waiting for transfers between devices, on_device(): lax.psum_scatter(partial_rows.astype(jnp.bfloat16), 'tensor', scatter_dim...  162 us
    all_gather x1, waiting for transfers between devices, on_device(): lax.all_gather(slot_rows.reshape(SPANS * CAP, model_width), 'tensor', axi...  160 us
    dot_general x1, matrix products, on_device(): jnp.dot(hidden, down_weight, preferred_element_type=jnp.float32)  18.5 us
    dot_general x1, matrix products, on_device(): jnp.dot(row_piece, gate_weight, preferred_element_type=jnp.float32)  11.1 us
    gather x1, local copies, waits for them, and re-layouts, on_device(): picked = jnp.take(expert_out, slot_index.reshape(-1), axis=0)  8.72 us
  transfers between devices with their start and end apart: 2, of which 2 were waited for; matrix products, arithmetic and copies ran while one was open for 0% of the time, Pallas kernels for 0%

commit v1 on v0

v1 whole, which is shorter than its diff:
```python
import jax
import jax.numpy as jnp
import numpy as np
from jax import lax
from jax.sharding import Mesh, PartitionSpec as P

SPANS = 4
CT = 128
CAP = 32
AXES = ("z_lo", "y", "core", "z_hi", "x")
SIZES = (2, 4, 2, 4, 4)
UNITS = 168
SPLIT = 1536
QUARTER = 768


def moved(value, target, sends=lambda z, y, core, x: True):
    pairs = []
    for source in range(int(np.prod(SIZES))):
        z_lo, y, core, z_hi, x = (int(i) for i in np.unravel_index(source, SIZES))
        z = 2 * z_hi + z_lo
        if sends(z, y, core, x):
            z, y, core, x = target(z, y, core, x)
            z, y, core, x = z % 8, y % 4, core % 2, x % 4
            pairs.append((source, int(np.ravel_multi_index((z % 2, y, core, z // 2, x), SIZES))))
    return lax.ppermute(value, AXES, pairs)


def along_z(z, y, core, x):
    return z + 1 - 2 * core, y, core, x


def along_y(z, y, core, x):
    return z, y + 1 - 2 * core, core, x


def other_core(z, y, core, x):
    return z, y, 1 - core, x


def along_x(step):
    return lambda z, y, core, x: (z, y, core, x + step)


def dot_rows(weight, rows):
    return lax.dot_general(weight, rows, (((1,), (1,)), ((), ())), preferred_element_type=jnp.float32)


def on_device(tokens, expert_ids, gate_probs, gate_weight, up_weight, down_weight):
    model_width = tokens.shape[1]
    z_lo, y, core, x = (lax.axis_index(name) for name in ("z_lo", "y", "core", "x"))
    first = z_lo != core
    half = y % 2

    is_window = expert_ids == 0
    routed = jnp.any(is_window, axis=1)
    gate_share = jnp.sum(jnp.where(is_window, gate_probs, 0.0), axis=1)
    routed_blocks = routed.reshape(SPANS, CT)
    slot_place = jnp.cumsum(routed_blocks.astype(jnp.int32), axis=1) - 1
    selector = (
        slot_place[:, None, :] == jnp.arange(CAP, dtype=jnp.int32)[None, :, None]
    ) & routed_blocks[:, None, :]
    slot_rows = jnp.einsum(
        "bst,btd->bsd",
        selector.astype(jnp.bfloat16),
        tokens.reshape(SPANS, CT, model_width),
        preferred_element_type=jnp.float32,
    ).astype(jnp.bfloat16)
    row_piece = lax.all_gather(slot_rows.reshape(SPANS * CAP, model_width), "x", axis=0, tiled=True)
    rows = jnp.concatenate([row_piece, moved(row_piece, other_core)], axis=0)
    rows_here = lax.dynamic_slice_in_dim(rows, half * SPLIT, SPLIT, 1)
    rows_there = lax.dynamic_slice_in_dim(rows, (1 - half) * SPLIT, SPLIT, 1)

    gate_t, up_t = gate_weight.T, up_weight.T
    near, far = core * UNITS, (1 - core) * UNITS

    def piece(array, start, side):
        return lax.dynamic_slice(array, (start, side * SPLIT), (UNITS, SPLIT))

    own = [
        piece(gate_t, near, half),
        piece(up_t, near, half),
        piece(down_weight, near, half),
        piece(gate_t, far, half),
        piece(up_t, far, half),
    ]
    own_down = piece(down_weight, far, half)

    from_z, from_y = [], []
    for step in range(11):
        if step < 5:
            feed = own[step]
        elif step < 7:
            feed = from_z[step - 3]
        elif step < 9:
            lanes = slice((step - 7) * QUARTER, (step - 6) * QUARTER)
            feed = jnp.concatenate([own_down[:, lanes], from_z[4][:, lanes]], axis=1)
        else:
            feed = None
        if step < 2:
            block, sends = feed, lambda z, y, core, x: z % 2 != core
            gets = lambda z, y, core, x: z % 2 == core
        elif feed is None:
            block, sends = from_z[step - 2], lambda z, y, core, x: z % 2 == core
            gets = lambda z, y, core, x: z % 2 != core
        else:
            block, sends = jnp.where(first, feed, from_z[step - 2]), lambda z, y, core, x: True
            gets = sends
        from_z.append(moved(block, along_z, sends))
        from_y.append(moved(from_z[step], along_y, gets))
    here = [jnp.where(first, from_z[i + 2], from_z[i]) for i in range(9)]
    there = [jnp.where(first, from_y[i + 2], from_y[i]) for i in range(9)]

    def hidden(gate_here, gate_there, up_here, up_there):
        gate_pre = dot_rows(gate_here, rows_here) + dot_rows(gate_there, rows_there)
        up_pre = dot_rows(up_here, rows_here) + dot_rows(up_there, rows_there)
        return (jax.nn.silu(gate_pre) * up_pre).astype(jnp.bfloat16)

    hidden_units = jnp.concatenate(
        [
            hidden(own[0], piece(gate_t, near, 1 - half), own[1], piece(up_t, near, 1 - half)),
            hidden(here[0], there[0], here[1], there[1]),
            hidden(here[3], there[3], here[4], there[4]),
            hidden(here[5], there[5], here[6], there[6]),
        ],
        axis=0,
    )

    def outputs(down_own, down_first, last):
        done = []
        for index in range(2):
            lanes = slice(index * QUARTER, (index + 1) * QUARTER)
            parts = [down_own[:, lanes], down_first[:, lanes], last[index][:, :QUARTER], last[index][:, QUARTER:]]
            down = jnp.concatenate(parts, axis=0)
            partial = lax.dot_general(
                hidden_units, down, (((0,), (0,)), ((), ())), preferred_element_type=jnp.float32
            )
            mine, others = partial[:512], partial[512:].astype(jnp.bfloat16)
            sums = mine + moved(others, other_core).astype(jnp.float32)
            sums = sums.astype(jnp.bfloat16).reshape(4, SPANS * CAP, QUARTER)
            total = lax.dynamic_index_in_dim(sums, x, 0, False).astype(jnp.float32)
            for step in (1, 3, 2):
                sent = lax.dynamic_index_in_dim(sums, (x + step) % 4, 0, False)
                total = total + moved(sent, along_x(step)).astype(jnp.float32)
            done.append(total)
        return jnp.concatenate(done, axis=1)

    out_here = outputs(own[2], here[2], here[7:9])
    out_there = outputs(piece(down_weight, near, 1 - half), there[2], there[7:9])
    low = half == 0
    expert_out = jnp.concatenate(
        [jnp.where(low, out_here, out_there), jnp.where(low, out_there, out_here)], axis=1
    ).reshape(SPANS, CAP, model_width)
    high_part = expert_out.astype(jnp.bfloat16)
    low_part = (expert_out - high_part.astype(jnp.float32)).astype(jnp.bfloat16)
    places = selector.astype(jnp.bfloat16)
    picked = jnp.einsum("bst,bsd->btd", places, high_part, preferred_element_type=jnp.float32)
    picked = picked + jnp.einsum("bst,bsd->btd", places, low_part, preferred_element_type=jnp.float32)
    mixed = gate_share[:, None] * picked.reshape(SPANS * CT, model_width)
    return mixed.astype(jnp.bfloat16)


def solution(mesh):
    grid = Mesh(mesh.devices.reshape(SIZES), AXES)
    shard = ("z_hi", "x")
    in_specs = (
        P(AXES, None),
        P(AXES, None),
        P(AXES, None),
        P(None, shard),
        P(None, shard),
        P(shard, None),
    )
    return jax.shard_map(
        on_device, mesh=grid, in_specs=in_specs, out_specs=P(AXES, None), check_vma=False
    )
```

time: 385 us -> 209 us (0.54)
  the two profiles are of different devices: /device:TPU:1 before, /device:TPU:112 now
where the time goes in v1:
time: 209 us; the launch traced here: 205 us
  starting transfers between devices  89.3 us (43%)
  waiting for transfers between devices  48.6 us (23%)
  matrix products  31.6 us (15%)
  between operations  14.3 us (7%)
  other arithmetic  12.3 us (6%)
  local copies, waits for them, and re-layouts  8.77 us (4%)
    ppermute x39, starting transfers between devices, moved(): return lax.ppermute(value, AXES, pairs)  89.3 us
    ppermute x39, waiting for transfers between devices, moved(): return lax.ppermute(value, AXES, pairs)  48.6 us
    dot_general x16, matrix products, dot_rows(): lax.dot_general(weight, rows, (((1,), (1,)), ((), ())), preferred_element...  22.3 us
    dot_general x4, matrix products, outputs(): lax.dot_general(hidden_units, down, (((0,), (0,)), ((), ())), preferred_e...  5.83 us
  transfers between devices with their start and end apart: 40, of which 19 were waited for; matrix products, arithmetic and copies ran while one was open for 21% of the time, Pallas kernels for 0%

profile of v1, /device:TPU:112, one launch (start us, length us, event | category | flops | bytes accessed | tf_op | source)
XLA Modules:
  0.0 204.9 jit_solution(16343133616173293361)
XLA Ops:
  6.5 2.0 dynamic-slice_bitcast_fusion.1
  8.5 5.8 %collective-permute-start.1 = (bf16[168,1536]{1,0:T(8,128)(2,1)}, bf16[168,1536]{1,0:T(8,128)(2,1)}, u32[]{:S(2)}, u32[]{:S(2)}) collective-permute-start(bf16[168,1536]{1,0:T(8,128)(2,1)} %dynamic-slice_bitcast_fusion.1), channel_id=1, source_target_pairs={{16,156},{17,157},{18,158},{19,159},{20,144},{21,145},{22,146},{23... | collective-permute-start | bytes 1548296 | tf_op jit(solution)/shard_map/ppermute | solution.py:26
  15.5 1.4 convolution_convert_fusion
  18.0 2.1 %collective-permute-start.5 = (bf16[168,1536]{1,0:T(8,128)(2,1)S(1)}, bf16[168,1536]{1,0:T(8,128)(2,1)}, u32[]{:S(2)}, u32[]{:S(2)}) collective-permute-start(bf16[168,1536]{1,0:T(8,128)(2,1)S(1)} %dynamic-slice_bitcast_fusion), channel_id=1, source_target_pairs={{16,156},{17,157},{18,158},{19,159},{20,144},{21,145},{22,146},{23... | collective-permute-start | bytes 1548296 | tf_op jit(solution)/shard_map/ppermute | solution.py:26
  21.7 3.9 %collective-permute-start.2 = (bf16[168,1536]{1,0:T(8,128)(2,1)S(1)}, bf16[168,1536]{1,0:T(8,128)(2,1)S(1)}, u32[]{:S(2)}, u32[]{:S(2)}) collective-permute-start(bf16[168,1536]{1,0:T(8,128)(2,1)S(1)} %dynamic-slice_select_fusion), channel_id=1, source_target_pairs={{0,128},{1,129},{2,130},{3,131},{4,132},{5,133},{6,134},{7,135},{8... | collective-permute-start | bytes 1548296 | tf_op jit(solution)/shard_map/ppermute | solution.py:26
  27.1 4.1 %collective-permute-start.6 = (bf16[168,1536]{1,0:T(8,128)(2,1)S(1)}, bf16[168,1536]{1,0:T(8,128)(2,1)S(1)}, u32[]{:S(2)}, u32[]{:S(2)}) collective-permute-start(bf16[168,1536]{1,0:T(8,128)(2,1)S(1)} %bitcast_select_fusion.1), channel_id=1, source_target_pairs={{0,128},{1,129},{2,130},{3,131},{4,132},{5,133},{6,134},{7,135},{8... | collective-permute-start | bytes 1548296 | tf_op jit(solution)/shard_map/ppermute | solution.py:26
  33.4 3.8 %collective-permute-start.11 = (bf16[168,1536]{1,0:T(8,128)(2,1)S(1)}, bf16[168,1536]{1,0:T(8,128)(2,1)S(1)}, u32[]{:S(2)}, u32[]{:S(2)}) collective-permute-start(bf16[168,1536]{1,0:T(8,128)(2,1)S(1)} %bitcast_select_fusion), channel_id=1, source_target_pairs={{0,128},{1,129},{2,130},{3,131},{4,132},{5,133},{6,134},{7,135},{8... | collective-permute-start | bytes 1548296 | tf_op jit(solution)/shard_map/ppermute | solution.py:26
  37.8 6.0 %collective-permute-done.11 = bf16[168,1536]{1,0:T(8,128)(2,1)S(1)} collective-permute-done((bf16[168,1536]{1,0:T(8,128)(2,1)S(1)}, bf16[168,1536]{1,0:T(8,128)(2,1)S(1)}, u32[]{:S(2)}, u32[]{:S(2)}) %collective-permute-start.11) | collective-permute-done | bytes 516128 | tf_op jit(solution)/shard_map/ppermute | solution.py:26
  44.9 3.7 %collective-permute-start.9 = (bf16[168,1536]{1,0:T(8,128)(2,1)}, bf16[168,1536]{1,0:T(8,128)(2,1)S(1)}, u32[]{:S(2)}, u32[]{:S(2)}) collective-permute-start(bf16[168,1536]{1,0:T(8,128)(2,1)} %get-tuple-element.32), channel_id=1, source_target_pairs={{0,128},{1,129},{2,130},{3,131},{4,132},{5,133},{6,134},{7,135},{8... | collective-permute-start | bytes 1548296 | tf_op jit(solution)/shard_map/ppermute | solution.py:26
  48.6 2.5 %fusion.142 = (bf16[168,768]{1,0:T(8,128)(2,1)}, bf16[168,768]{1,0:T(8,128)(2,1)}, bf16[168,768]{1,0:T(8,128)(2,1)}, bf16[168,768]{1,0:T(8,128)(2,1)S(1)}, bf16[...) fusion(bf16[336,3072]{1,0:T(8,128)(2,1)} %param.11, s32[]{:T(128)S(6)} %select_n.216, s32[]{:T(128)S(6)} %select_n.215, ...), kind=kLoop, calls=%fused_computation.199 | loop fusion | bytes 3096600 | tf_op jit(solution)/shard_map/slice | solution.py:133
  51.0 1.5 collective-permute-start.4
  54.5 1.6 collective-permute-start.14
  56.3 3.0 %collective-permute-start.15 = (bf16[168,1536]{1,0:T(8,128)(2,1)S(1)}, bf16[168,1536]{1,0:T(8,128)(2,1)}, u32[]{:S(2)}, u32[]{:S(2)}) collective-permute-start(bf16[168,1536]{1,0:T(8,128)(2,1)S(1)} %maximum_select_fusion), channel_id=1, source_target_pairs={{0,128},{1,129},{2,130},{3,131},{4,132},{5,133},{6,134},{7,135},{8... | collective-permute-start | bytes 1548296 | tf_op jit(solution)/shard_map/ppermute | solution.py:26
  59.3 3.6 %collective-permute-done.12 = bf16[168,1536]{1,0:T(8,128)(2,1)S(1)} collective-permute-done((bf16[168,1536]{1,0:T(8,128)(2,1)S(1)}, bf16[168,1536]{1,0:T(8,128)(2,1)S(1)}, u32[]{:S(2)}, u32[]{:S(2)}) %collective-permute-start.12) | collective-permute-done | bytes 516128 | tf_op jit(solution)/shard_map/ppermute | solution.py:26
  63.0 2.1 %collective-permute-start.17 = (bf16[168,1536]{1,0:T(8,128)(2,1)S(1)}, bf16[168,1536]{1,0:T(8,128)(2,1)}, u32[]{:S(2)}, u32[]{:S(2)}) collective-permute-start(bf16[168,1536]{1,0:T(8,128)(2,1)S(1)} %maximum_select_fusion.1), channel_id=1, source_target_pairs={{0,128},{1,129},{2,130},{3,131},{4,132},{5,133},{6,134},{7,135},{8... | collective-permute-start | bytes 1548296 | tf_op jit(solution)/shard_map/ppermute | solution.py:26
  65.9 1.5 collective-permute-start.8
  68.5 1.3 collective-permute-start.19
  69.9 4.1 %collective-permute-done.17 = bf16[168,1536]{1,0:T(8,128)(2,1)} collective-permute-done((bf16[168,1536]{1,0:T(8,128)(2,1)S(1)}, bf16[168,1536]{1,0:T(8,128)(2,1)}, u32[]{:S(2)}, u32[]{:S(2)}) %collective-permute-start.17) | collective-permute-done | bytes 516128 | tf_op jit(solution)/shard_map/ppermute | solution.py:26
  76.4 3.4 %collective-permute-done.19 = bf16[168,1536]{1,0:T(8,128)(2,1)} collective-permute-done((bf16[168,1536]{1,0:T(8,128)(2,1)}, bf16[168,1536]{1,0:T(8,128)(2,1)}, u32[]{:S(2)}, u32[]{:S(2)}) %collective-permute-start.19) | collective-permute-done | bytes 516128 | tf_op jit(solution)/shard_map/ppermute | solution.py:26
  80.9 4.4 %collective-permute-done.24 = bf16[168,1536]{1,0:T(8,128)(2,1)} collective-permute-done((bf16[168,1536]{1,0:T(8,128)(2,1)}, bf16[168,1536]{1,0:T(8,128)(2,1)}, u32[]{:S(2)}, u32[]{:S(2)}) %collective-permute-start.24) | collective-permute-done | bytes 516128 | tf_op jit(solution)/shard_map/ppermute | solution.py:26
  85.3 2.4 %collective-permute-start.29 = (bf16[168,1536]{1,0:T(8,128)(2,1)}, bf16[168,1536]{1,0:T(8,128)(2,1)S(1)}, u32[]{:S(2)}, u32[]{:S(2)}) collective-permute-start(bf16[168,1536]{1,0:T(8,128)(2,1)} %collective-permute-done.19), channel_id=1, source_target_pairs={{16,112},{17,113},{18,114},{19,115},{20,116},{21,117},{22,118},{23... | collective-permute-start | bytes 1548296 | tf_op jit(solution)/shard_map/ppermute | solution.py:26
  88.9 1.7 collective-permute-start.18
  90.6 5.9 %collective-permute-done.29 = bf16[168,1536]{1,0:T(8,128)(2,1)S(1)} collective-permute-done((bf16[168,1536]{1,0:T(8,128)(2,1)}, bf16[168,1536]{1,0:T(8,128)(2,1)S(1)}, u32[]{:S(2)}, u32[]{:S(2)}) %collective-permute-start.29) | collective-permute-done | bytes 516128 | tf_op jit(solution)/shard_map/ppermute | solution.py:26
  96.5 12.9 %collective-permute-start.34 = (bf16[168,1536]{1,0:T(8,128)(2,1)}, bf16[168,1536]{1,0:T(8,128)(2,1)S(1)}, u32[]{:S(2)}, u32[]{:S(2)}) collective-permute-start(bf16[168,1536]{1,0:T(8,128)(2,1)} %collective-permute-done.24), channel_id=1, source_target_pairs={{16,112},{17,113},{18,114},{19,115},{20,116},{21,117},{22,118},{23... | collective-permute-start | bytes 1548296 | tf_op jit(solution)/shard_map/ppermute | solution.py:26
  109.5 2.9 %collective-permute-start.7 = (bf16[168,1536]{1,0:T(8,128)(2,1)S(1)}, bf16[168,1536]{1,0:T(8,128)(2,1)S(1)}, u32[]{:S(2)}, u32[]{:S(2)}) collective-permute-start(bf16[168,1536]{1,0:T(8,128)(2,1)S(1)} %collective-permute-done.6), channel_id=1, source_target_pairs={{0,32},{1,33},{2,34},{3,35},{4,36},{5,37},{6,38},{7,39},{8,40},{9,... | collective-permute-start | bytes 1548296 | tf_op jit(solution)/shard_map/ppermute | solution.py:26
  112.4 5.8 %collective-permute-done.34 = bf16[168,1536]{1,0:T(8,128)(2,1)S(1)} collective-permute-done((bf16[168,1536]{1,0:T(8,128)(2,1)}, bf16[168,1536]{1,0:T(8,128)(2,1)S(1)}, u32[]{:S(2)}, u32[]{:S(2)}) %collective-permute-start.34) | collective-permute-done | bytes 516128 | tf_op jit(solution)/shard_map/ppermute | solution.py:26
  119.4 3.7 %collective-permute-start.13 = (bf16[168,1536]{1,0:T(8,128)(2,1)S(1)}, bf16[168,1536]{1,0:T(8,128)(2,1)S(1)}, u32[]{:S(2)}, u32[]{:S(2)}) collective-permute-start(bf16[168,1536]{1,0:T(8,128)(2,1)S(1)} %collective-permute-done.12), channel_id=1, source_target_pairs={{0,32},{1,33},{2,34},{3,35},{4,36},{5,37},{6,38},{7,39},{8,40},{9,... | collective-permute-start | bytes 1548296 | tf_op jit(solution)/shard_map/ppermute | solution.py:26
  130.7 2.3 %fusion.60 = f32[168,1024]{1,0:T(8,128)S(1)} fusion(bf16[1024,3072]{1,0:T(8,128)(2,1)S(1)} %constant_dynamic-update-slice_fusion, s32[]{:T(128)S(6)} %select_n.215, bf16[168,1536]{1,0:T(8,128)(2,1)} %collective-permute-done.15, bf16[168,1536]{1,0:T(8,128)(2,1)S(1)} %collective-permute-done.9, pred[]{:T(512)S(6)} %ne.40), kind=kOutput, calls=%fused_computation.84 | convolution fusion | flops 528740352 | bytes 4866053 | tf_op jit(solution)/shard_map/dot_general | solution.py:46
  139.6 1.3 fusion.10
  140.9 2.7 %fusion.58 = f32[168,1024]{1,0:T(8,128)S(1)} fusion(bf16[1024,3072]{1,0:T(8,128)(2,1)S(1)} %constant_dynamic-update-slice_fusion, s32[]{:T(128)S(6)} %select_n.215, bf16[168,1536]{1,0:T(8,128)(2,1)} %collective-permute-done.17, bf16[168,1536]{1,0:T(8,128)(2,1)S(1)} %collective-permute-done.12, pred[]{:T(512)S(6)} %ne.40), kind=kOutput, calls=%fused_computation.82 | convolution fusion | flops 528740352 | bytes 4866053 | tf_op jit(solution)/shard_map/dot_general | solution.py:46
  144.9 1.3 fusion.9
  146.3 1.5 fusion.12
  148.0 1.5 fusion.20
  150.1 1.5 fusion.28
  151.8 1.5 fusion.36
  154.1 1.6 collective-permute-start.21
  155.7 1.7 collective-permute-start.22
  157.4 2.0 collective-permute-start.23
  160.5 2.7 %collective-permute-start.27 = (bf16[128,768]{1,0:T(8,128)(2,1)S(1)}, bf16[128,768]{1,0:T(8,128)(2,1)S(1)}, u32[]{:S(2)}, u32[]{:S(2)}) collective-permute-start(bf16[128,768]{1,0:T(8,128)(2,1)S(1)} %get-tuple-element.20), channel_id=1, source_target_pairs={{0,3},{1,0},{2,1},{3,2},{4,7},{5,4},{6,5},{7,6},{8,11},{9,8},{10,9... | collective-permute-start | bytes 589832 | tf_op jit(solution)/shard_map/ppermute | solution.py:26
  163.5 5.4 %collective-permute-start.28 = (bf16[128,768]{1,0:T(8,128)(2,1)S(1)}, bf16[128,768]{1,0:T(8,128)(2,1)S(1)}, u32[]{:S(2)}, u32[]{:S(2)}) collective-permute-start(bf16[128,768]{1,0:T(8,128)(2,1)S(1)} %get-tuple-element.19), channel_id=1, source_target_pairs={{0,2},{1,3},{2,0},{3,1},{4,6},{5,7},{6,4},{7,5},{8,10},{9,11},{10,... | collective-permute-start | bytes 589832 | tf_op jit(solution)/shard_map/ppermute | solution.py:26
  168.9 3.2 %collective-permute-start.32 = (bf16[128,768]{1,0:T(8,128)(2,1)S(1)}, bf16[128,768]{1,0:T(8,128)(2,1)S(1)}, u32[]{:S(2)}, u32[]{:S(2)}) collective-permute-start(bf16[128,768]{1,0:T(8,128)(2,1)S(1)} %get-tuple-element.23), channel_id=1, source_target_pairs={{0,3},{1,0},{2,1},{3,2},{4,7},{5,4},{6,5},{7,6},{8,11},{9,8},{10,9... | collective-permute-start | bytes 589832 | tf_op jit(solution)/shard_map/ppermute | solution.py:26
  172.3 2.9 %collective-permute-done.26 = bf16[128,768]{1,0:T(8,128)(2,1)S(1)} collective-permute-done((bf16[128,768]{1,0:T(8,128)(2,1)S(1)}, bf16[128,768]{1,0:T(8,128)(2,1)S(1)}, u32[]{:S(2)}, u32[]{:S(2)}) %collective-permute-start.26) | collective-permute-done | bytes 196640 | tf_op jit(solution)/shard_map/ppermute | solution.py:26
  175.2 1.5 collective-permute-start.33
  176.9 3.1 %collective-permute-start.37 = (bf16[128,768]{1,0:T(8,128)(2,1)S(1)}, bf16[128,768]{1,0:T(8,128)(2,1)S(1)}, u32[]{:S(2)}, u32[]{:S(2)}) collective-permute-start(bf16[128,768]{1,0:T(8,128)(2,1)S(1)} %get-tuple-element.26), channel_id=1, source_target_pairs={{0,3},{1,0},{2,1},{3,2},{4,7},{5,4},{6,5},{7,6},{8,11},{9,8},{10,9... | collective-permute-start | bytes 589832 | tf_op jit(solution)/shard_map/ppermute | solution.py:26
  181.2 3.9 %collective-permute-start.38 = (bf16[128,768]{1,0:T(8,128)(2,1)S(1)}, bf16[128,768]{1,0:T(8,128)(2,1)S(1)}, u32[]{:S(2)}, u32[]{:S(2)}) collective-permute-start(bf16[128,768]{1,0:T(8,128)(2,1)S(1)} %get-tuple-element.25), channel_id=1, source_target_pairs={{0,2},{1,3},{2,0},{3,1},{4,6},{5,7},{6,4},{7,5},{8,10},{9,11},{10,... | collective-permute-start | bytes 589832 | tf_op jit(solution)/shard_map/ppermute | solution.py:26
  185.4 2.4 %collective-permute-done.36 = bf16[128,768]{1,0:T(8,128)(2,1)S(1)} collective-permute-done((bf16[128,768]{1,0:T(8,128)(2,1)S(1)}, bf16[128,768]{1,0:T(8,128)(2,1)S(1)}, u32[]{:S(2)}, u32[]{:S(2)}) %collective-permute-start.36) | collective-permute-done | bytes 196640 | tf_op jit(solution)/shard_map/ppermute | solution.py:26
  188.9 3.9 %collective-permute-done.38 = bf16[128,768]{1,0:T(8,128)(2,1)S(1)} collective-permute-done((bf16[128,768]{1,0:T(8,128)(2,1)S(1)}, bf16[128,768]{1,0:T(8,128)(2,1)S(1)}, u32[]{:S(2)}, u32[]{:S(2)}) %collective-permute-start.38) | collective-permute-done | bytes 196640 | tf_op jit(solution)/shard_map/ppermute | solution.py:26
  195.2 2.7 %fusion = bf16[512,3072]{1,0:T(8,128)(2,1)} fusion(f32[4,128,3072]{2,1,0:T(8,128)S(1)} %convolution_add_fusion, f32[512]{0:T(512)S(1)} %get-tuple-element.5), kind=kLoop, calls=%fused_computation.1 | loop fusion | flops 3145728 | bytes 9439232 | tf_op jit(solution)/shard_map/convert_element_type | solution.py:160
  (140 shorter events, 43.5 us)
Async XLA Ops:
  6.5 8.9 %copy-start = (bf16[512,3072]{1,0:T(8,128)(2,1)S(1)}, bf16[512,3072]{1,0:T(8,128)(2,1)}, u32[]{:S(2)}) copy-start(bf16[512,3072]{1,0:T(8,128)(2,1)} %param.6) | copy-start | bytes 9437188
  6.5 73.3 %all-gather.2.cloned.1.call-start = ((), (), s32[]{:S(2)}) async-start(), calls=%async_computation | async-start | bytes 3932160 | tf_op jit(solution)/shard_map/all_gather | solution.py:69
  8.5 11.9 %collective-permute-start.1 = (bf16[168,1536]{1,0:T(8,128)(2,1)}, bf16[168,1536]{1,0:T(8,128)(2,1)}, u32[]{:S(2)}, u32[]{:S(2)}) collective-permute-start(bf16[168,1536]{1,0:T(8,128)(2,1)} %dynamic-slice_bitcast_fusion.1), channel_id=1, source_target_pairs={{16,156},{17,157},{18,158},{19,159},{20,144},{21,145},{22,146},{23... | collective-permute-start | bytes 1548296 | tf_op jit(solution)/shard_map/ppermute | solution.py:26
  18.0 7.9 %collective-permute-start.5 = (bf16[168,1536]{1,0:T(8,128)(2,1)S(1)}, bf16[168,1536]{1,0:T(8,128)(2,1)}, u32[]{:S(2)}, u32[]{:S(2)}) collective-permute-start(bf16[168,1536]{1,0:T(8,128)(2,1)S(1)} %dynamic-slice_bitcast_fusion), channel_id=1, source_target_pairs={{16,156},{17,157},{18,158},{19,159},{20,144},{21,145},{22,146},{23... | collective-permute-start | bytes 1548296 | tf_op jit(solution)/shard_map/ppermute | solution.py:26
  21.7 10.5 %collective-permute-start.2 = (bf16[168,1536]{1,0:T(8,128)(2,1)S(1)}, bf16[168,1536]{1,0:T(8,128)(2,1)S(1)}, u32[]{:S(2)}, u32[]{:S(2)}) collective-permute-start(bf16[168,1536]{1,0:T(8,128)(2,1)S(1)} %dynamic-slice_select_fusion), channel_id=1, source_target_pairs={{0,128},{1,129},{2,130},{3,131},{4,132},{5,133},{6,134},{7,135},{8... | collective-permute-start | bytes 1548296 | tf_op jit(solution)/shard_map/ppermute | solution.py:26
  27.1 10.7 %collective-permute-start.6 = (bf16[168,1536]{1,0:T(8,128)(2,1)S(1)}, bf16[168,1536]{1,0:T(8,128)(2,1)S(1)}, u32[]{:S(2)}, u32[]{:S(2)}) collective-permute-start(bf16[168,1536]{1,0:T(8,128)(2,1)S(1)} %bitcast_select_fusion.1), channel_id=1, source_target_pairs={{0,128},{1,129},{2,130},{3,131},{4,132},{5,133},{6,134},{7,135},{8... | collective-permute-start | bytes 1548296 | tf_op jit(solution)/shard_map/ppermute | solution.py:26
  33.4 10.4 %collective-permute-start.11 = (bf16[168,1536]{1,0:T(8,128)(2,1)S(1)}, bf16[168,1536]{1,0:T(8,128)(2,1)S(1)}, u32[]{:S(2)}, u32[]{:S(2)}) collective-permute-start(bf16[168,1536]{1,0:T(8,128)(2,1)S(1)} %bitcast_select_fusion), channel_id=1, source_target_pairs={{0,128},{1,129},{2,130},{3,131},{4,132},{5,133},{6,134},{7,135},{8... | collective-permute-start | bytes 1548296 | tf_op jit(solution)/shard_map/ppermute | solution.py:26
  44.9 11.3 %collective-permute-start.9 = (bf16[168,1536]{1,0:T(8,128)(2,1)}, bf16[168,1536]{1,0:T(8,128)(2,1)S(1)}, u32[]{:S(2)}, u32[]{:S(2)}) collective-permute-start(bf16[168,1536]{1,0:T(8,128)(2,1)} %get-tuple-element.32), channel_id=1, source_target_pairs={{0,128},{1,129},{2,130},{3,131},{4,132},{5,133},{6,134},{7,135},{8... | collective-permute-start | bytes 1548296 | tf_op jit(solution)/shard_map/ppermute | solution.py:26
  48.6 5.2 %copy-start.9 = (bf16[168,1536]{1,0:T(8,128)(2,1)S(1)}, bf16[168,1536]{1,0:T(8,128)(2,1)}, u32[]{:S(2)}) copy-start(bf16[168,1536]{1,0:T(8,128)(2,1)} %get-tuple-element.33) | copy-start | bytes 1548292
  51.0 77.2 %collective-permute-start.4 = (bf16[168,1536]{1,0:T(8,128)(2,1)}, bf16[168,1536]{1,0:T(8,128)(2,1)}, u32[]{:S(2)}, u32[]{:S(2)}) collective-permute-start(bf16[168,1536]{1,0:T(8,128)(2,1)} %collective-permute-done.1), channel_id=1, source_target_pairs={{0,32},{1,33},{2,34},{3,35},{4,36},{5,37},{6,38},{7,39},{8,40},{9,... | collective-permute-start | bytes 1548296 | tf_op jit(solution)/shard_map/ppermute | solution.py:26
  52.5 13.4 %collective-permute-start.3 = (bf16[168,1536]{1,0:T(8,128)(2,1)S(1)}, bf16[168,1536]{1,0:T(8,128)(2,1)S(1)}, u32[]{:S(2)}, u32[]{:S(2)}) collective-permute-start(bf16[168,1536]{1,0:T(8,128)(2,1)S(1)} %collective-permute-done.2), channel_id=1, source_target_pairs={{0,32},{1,33},{2,34},{3,35},{4,36},{5,37},{6,38},{7,39},{8,40},{9,... | collective-permute-start | bytes 1548296 | tf_op jit(solution)/shard_map/ppermute | solution.py:26
  53.8 9.1 %collective-permute-start.12 = (bf16[168,1536]{1,0:T(8,128)(2,1)S(1)}, bf16[168,1536]{1,0:T(8,128)(2,1)S(1)}, u32[]{:S(2)}, u32[]{:S(2)}) collective-permute-start(bf16[168,1536]{1,0:T(8,128)(2,1)S(1)} %copy-done.9), channel_id=1, source_target_pairs={{0,128},{1,129},{2,130},{3,131},{4,132},{5,133},{6,134},{7,135},{8... | collective-permute-start | bytes 1548296 | tf_op jit(solution)/shard_map/ppermute | solution.py:26
  54.5 15.3 %collective-permute-start.14 = (bf16[168,1536]{1,0:T(8,128)(2,1)S(1)}, bf16[168,1536]{1,0:T(8,128)(2,1)S(1)}, u32[]{:S(2)}, u32[]{:S(2)}) collective-permute-start(bf16[168,1536]{1,0:T(8,128)(2,1)S(1)} %collective-permute-done.11), channel_id=1, source_target_pairs={{0,32},{1,33},{2,34},{3,35},{4,36},{5,37},{6,38},{7,39},{8,40},{9,... | collective-permute-start | bytes 1548296 | tf_op jit(solution)/shard_map/ppermute | solution.py:26
  56.3 12.2 %collective-permute-start.15 = (bf16[168,1536]{1,0:T(8,128)(2,1)S(1)}, bf16[168,1536]{1,0:T(8,128)(2,1)}, u32[]{:S(2)}, u32[]{:S(2)}) collective-permute-start(bf16[168,1536]{1,0:T(8,128)(2,1)S(1)} %maximum_select_fusion), channel_id=1, source_target_pairs={{0,128},{1,129},{2,130},{3,131},{4,132},{5,133},{6,134},{7,135},{8... | collective-permute-start | bytes 1548296 | tf_op jit(solution)/shard_map/ppermute | solution.py:26
  63.0 11.0 %collective-permute-start.17 = (bf16[168,1536]{1,0:T(8,128)(2,1)S(1)}, bf16[168,1536]{1,0:T(8,128)(2,1)}, u32[]{:S(2)}, u32[]{:S(2)}) collective-permute-start(bf16[168,1536]{1,0:T(8,128)(2,1)S(1)} %maximum_select_fusion.1), channel_id=1, source_target_pairs={{0,128},{1,129},{2,130},{3,131},{4,132},{5,133},{6,134},{7,135},{8... | collective-permute-start | bytes 1548296 | tf_op jit(solution)/shard_map/ppermute | solution.py:26
  65.9 3.9 %copy-start.4 = (bf16[168,1536]{1,0:T(8,128)(2,1)}, bf16[168,1536]{1,0:T(8,128)(2,1)S(1)}, u32[]{:S(2)}) copy-start(bf16[168,1536]{1,0:T(8,128)(2,1)S(1)} %collective-permute-done.3) | copy-start | bytes 1548292
  65.9 79.0 %collective-permute-start.8 = (bf16[168,1536]{1,0:T(8,128)(2,1)}, bf16[168,1536]{1,0:T(8,128)(2,1)}, u32[]{:S(2)}, u32[]{:S(2)}) collective-permute-start(bf16[168,1536]{1,0:T(8,128)(2,1)} %collective-permute-done.5), channel_id=1, source_target_pairs={{0,32},{1,33},{2,34},{3,35},{4,36},{5,37},{6,38},{7,39},{8,40},{9,... | collective-permute-start | bytes 1548296 | tf_op jit(solution)/shard_map/ppermute | solution.py:26
  68.5 11.3 %collective-permute-start.19 = (bf16[168,1536]{1,0:T(8,128)(2,1)}, bf16[168,1536]{1,0:T(8,128)(2,1)}, u32[]{:S(2)}, u32[]{:S(2)}) collective-permute-start(bf16[168,1536]{1,0:T(8,128)(2,1)} %collective-permute-done.15), channel_id=1, source_target_pairs={{0,128},{1,129},{2,130},{3,131},{4,132},{5,133},{6,134},{7,135},{8... | collective-permute-start | bytes 1548296 | tf_op jit(solution)/shard_map/ppermute | solution.py:26
  69.8 6.3 %copy-start.10 = (bf16[168,1536]{1,0:T(8,128)(2,1)}, bf16[168,1536]{1,0:T(8,128)(2,1)S(1)}, u32[]{:S(2)}) copy-start(bf16[168,1536]{1,0:T(8,128)(2,1)S(1)} %collective-permute-done.14) | copy-start | bytes 1548292
  74.0 11.3 %collective-permute-start.24 = (bf16[168,1536]{1,0:T(8,128)(2,1)}, bf16[168,1536]{1,0:T(8,128)(2,1)}, u32[]{:S(2)}, u32[]{:S(2)}) collective-permute-start(bf16[168,1536]{1,0:T(8,128)(2,1)} %collective-permute-done.17), channel_id=1, source_target_pairs={{0,128},{1,129},{2,130},{3,131},{4,132},{5,133},{6,134},{7,135},{8... | collective-permute-start | bytes 1548296 | tf_op jit(solution)/shard_map/ppermute | solution.py:26
  76.1 12.8 %collective-permute-start.16 = (bf16[168,1536]{1,0:T(8,128)(2,1)}, bf16[168,1536]{1,0:T(8,128)(2,1)S(1)}, u32[]{:S(2)}, u32[]{:S(2)}) collective-permute-start(bf16[168,1536]{1,0:T(8,128)(2,1)} %collective-permute-done.15), channel_id=1, source_target_pairs={{0,32},{1,33},{2,34},{3,35},{4,36},{5,37},{6,38},{7,39},{8,40},{9,... | collective-permute-start | bytes 1548296 | tf_op jit(solution)/shard_map/ppermute | solution.py:26
  79.8 39.6 %collective-permute-start = (bf16[512,3072]{1,0:T(8,128)(2,1)}, bf16[512,3072]{1,0:T(8,128)(2,1)S(1)}, u32[]{:S(2)}, u32[]{:S(2)}) collective-permute-start(bf16[512,3072]{1,0:T(8,128)(2,1)} %all-gather.2.cloned.1.call-done), channel_id=1, source_target_pairs={{0,16},{1,17},{2,18},{3,19},{4,20},{5,21},{6,22},{7,23},{8,24},{9,... | collective-permute-start | bytes 9437192 | tf_op jit(solution)/shard_map/ppermute | solution.py:26
  85.3 11.2 %collective-permute-start.29 = (bf16[168,1536]{1,0:T(8,128)(2,1)}, bf16[168,1536]{1,0:T(8,128)(2,1)S(1)}, u32[]{:S(2)}, u32[]{:S(2)}) collective-permute-start(bf16[168,1536]{1,0:T(8,128)(2,1)} %collective-permute-done.19), channel_id=1, source_target_pairs={{16,112},{17,113},{18,114},{19,115},{20,116},{21,117},{22,118},{23... | collective-permute-start | bytes 1548296 | tf_op jit(solution)/shard_map/ppermute | solution.py:26
  88.9 30.3 %copy-start.2 = (bf16[512,3072]{1,0:T(8,128)(2,1)S(1)}, bf16[512,3072]{1,0:T(8,128)(2,1)}, u32[]{:S(2)}) copy-start(bf16[512,3072]{1,0:T(8,128)(2,1)} %all-gather.2.cloned.1.call-done) | copy-start | bytes 9437188
  88.9 23.5 %copy-start.6 = (bf16[168,1536]{1,0:T(8,128)(2,1)}, bf16[168,1536]{1,0:T(8,128)(2,1)S(1)}, u32[]{:S(2)}) copy-start(bf16[168,1536]{1,0:T(8,128)(2,1)S(1)} %collective-permute-done.16) | copy-start | bytes 1548292
  88.9 20.6 %collective-permute-start.18 = (bf16[168,1536]{1,0:T(8,128)(2,1)}, bf16[168,1536]{1,0:T(8,128)(2,1)S(1)}, u32[]{:S(2)}, u32[]{:S(2)}) collective-permute-start(bf16[168,1536]{1,0:T(8,128)(2,1)} %collective-permute-done.17), channel_id=1, source_target_pairs={{0,32},{1,33},{2,34},{3,35},{4,36},{5,37},{6,38},{7,39},{8,40},{9,... | collective-permute-start | bytes 1548296 | tf_op jit(solution)/shard_map/ppermute | solution.py:26
  96.5 21.7 %collective-permute-start.34 = (bf16[168,1536]{1,0:T(8,128)(2,1)}, bf16[168,1536]{1,0:T(8,128)(2,1)S(1)}, u32[]{:S(2)}, u32[]{:S(2)}) collective-permute-start(bf16[168,1536]{1,0:T(8,128)(2,1)} %collective-permute-done.24), channel_id=1, source_target_pairs={{16,112},{17,113},{18,114},{19,115},{20,116},{21,117},{22,118},{23... | collective-permute-start | bytes 1548296 | tf_op jit(solution)/shard_map/ppermute | solution.py:26
  109.5 24.8 %collective-permute-start.7 = (bf16[168,1536]{1,0:T(8,128)(2,1)S(1)}, bf16[168,1536]{1,0:T(8,128)(2,1)S(1)}, u32[]{:S(2)}, u32[]{:S(2)}) collective-permute-start(bf16[168,1536]{1,0:T(8,128)(2,1)S(1)} %collective-permute-done.6), channel_id=1, source_target_pairs={{0,32},{1,33},{2,34},{3,35},{4,36},{5,37},{6,38},{7,39},{8,40},{9,... | collective-permute-start | bytes 1548296 | tf_op jit(solution)/shard_map/ppermute | solution.py:26
  118.2 14.8 %collective-permute-start.10 = (bf16[168,1536]{1,0:T(8,128)(2,1)S(1)}, bf16[168,1536]{1,0:T(8,128)(2,1)S(1)}, u32[]{:S(2)}, u32[]{:S(2)}) collective-permute-start(bf16[168,1536]{1,0:T(8,128)(2,1)S(1)} %collective-permute-done.9), channel_id=1, source_target_pairs={{0,32},{1,33},{2,34},{3,35},{4,36},{5,37},{6,38},{7,39},{8,40},{9,... | collective-permute-start | bytes 1548296 | tf_op jit(solution)/shard_map/ppermute | solution.py:26
  119.4 3.9 %copy-start.3 = (bf16[3072,336]{0,1:T(8,128)(2,1)S(1)}, bf16[3072,336]{0,1:T(8,128)(2,1)}, u32[]{:S(2)}) copy-start(bf16[3072,336]{0,1:T(8,128)(2,1)} %param.9) | copy-start | bytes 6193156
  119.4 20.2 %collective-permute-start.13 = (bf16[168,1536]{1,0:T(8,128)(2,1)S(1)}, bf16[168,1536]{1,0:T(8,128)(2,1)S(1)}, u32[]{:S(2)}, u32[]{:S(2)}) collective-permute-start(bf16[168,1536]{1,0:T(8,128)(2,1)S(1)} %collective-permute-done.12), channel_id=1, source_target_pairs={{0,32},{1,33},{2,34},{3,35},{4,36},{5,37},{6,38},{7,39},{8,40},{9,... | collective-permute-start | bytes 1548296 | tf_op jit(solution)/shard_map/ppermute | solution.py:26
  147.8 6.1 %collective-permute-start.20 = (bf16[512,768]{1,0:T(8,128)(2,1)S(1)}, bf16[512,768]{1,0:T(8,128)(2,1)S(1)}, u32[]{:S(2)}, u32[]{:S(2)}) collective-permute-start(bf16[512,768]{1,0:T(8,128)(2,1)S(1)} %slice.157), channel_id=1, source_target_pairs={{0,16},{1,17},{2,18},{3,19},{4,20},{5,21},{6,22},{7,23},{8,24},{9,... | collective-permute-start | bytes 2359304 | tf_op jit(solution)/shard_map/ppermute | solution.py:26
  149.5 7.9 %collective-permute-start.25 = (bf16[512,768]{1,0:T(8,128)(2,1)S(1)}, bf16[512,768]{1,0:T(8,128)(2,1)S(1)}, u32[]{:S(2)}, u32[]{:S(2)}) collective-permute-start(bf16[512,768]{1,0:T(8,128)(2,1)S(1)} %slice.156), channel_id=1, source_target_pairs={{0,16},{1,17},{2,18},{3,19},{4,20},{5,21},{6,22},{7,23},{8,24},{9,... | collective-permute-start | bytes 2359304 | tf_op jit(solution)/shard_map/ppermute | solution.py:26
  151.6 8.0 %collective-permute-start.30 = (bf16[512,768]{1,0:T(8,128)(2,1)S(1)}, bf16[512,768]{1,0:T(8,128)(2,1)S(1)}, u32[]{:S(2)}, u32[]{:S(2)}) collective-permute-start(bf16[512,768]{1,0:T(8,128)(2,1)S(1)} %slice.155), channel_id=1, source_target_pairs={{0,16},{1,17},{2,18},{3,19},{4,20},{5,21},{6,22},{7,23},{8,24},{9,... | collective-permute-start | bytes 2359304 | tf_op jit(solution)/shard_map/ppermute | solution.py:26
  153.3 7.1 %collective-permute-start.35 = (bf16[512,768]{1,0:T(8,128)(2,1)S(1)}, bf16[512,768]{1,0:T(8,128)(2,1)S(1)}, u32[]{:S(2)}, u32[]{:S(2)}) collective-permute-start(bf16[512,768]{1,0:T(8,128)(2,1)S(1)} %slice.154), channel_id=1, source_target_pairs={{0,16},{1,17},{2,18},{3,19},{4,20},{5,21},{6,22},{7,23},{8,24},{9,... | collective-permute-start | bytes 2359304 | tf_op jit(solution)/shard_map/ppermute | solution.py:26
  154.1 9.4 %collective-permute-start.21 = (bf16[128,768]{1,0:T(8,128)(2,1)S(1)}, bf16[128,768]{1,0:T(8,128)(2,1)S(1)}, u32[]{:S(2)}, u32[]{:S(2)}) collective-permute-start(bf16[128,768]{1,0:T(8,128)(2,1)S(1)} %get-tuple-element.15), channel_id=1, source_target_pairs={{0,1},{1,2},{2,3},{3,0},{4,5},{5,6},{6,7},{7,4},{8,9},{9,10},{10,1... | collective-permute-start | bytes 589832 | tf_op jit(solution)/shard_map/ppermute | solution.py:26
  155.7 13.3 %collective-permute-start.22 = (bf16[128,768]{1,0:T(8,128)(2,1)S(1)}, bf16[128,768]{1,0:T(8,128)(2,1)S(1)}, u32[]{:S(2)}, u32[]{:S(2)}) collective-permute-start(bf16[128,768]{1,0:T(8,128)(2,1)S(1)} %get-tuple-element.17), channel_id=1, source_target_pairs={{0,3},{1,0},{2,1},{3,2},{4,7},{5,4},{6,5},{7,6},{8,11},{9,8},{10,9... | collective-permute-start | bytes 589832 | tf_op jit(solution)/shard_map/ppermute | solution.py:26
  157.4 11.5 %collective-permute-start.23 = (bf16[128,768]{1,0:T(8,128)(2,1)S(1)}, bf16[128,768]{1,0:T(8,128)(2,1)S(1)}, u32[]{:S(2)}, u32[]{:S(2)}) collective-permute-start(bf16[128,768]{1,0:T(8,128)(2,1)S(1)} %get-tuple-element.16), channel_id=1, source_target_pairs={{0,2},{1,3},{2,0},{3,1},{4,6},{5,7},{6,4},{7,5},{8,10},{9,11},{10,... | collective-permute-start | bytes 589832 | tf_op jit(solution)/shard_map/ppermute | solution.py:26
  159.6 15.5 %collective-permute-start.26 = (bf16[128,768]{1,0:T(8,128)(2,1)S(1)}, bf16[128,768]{1,0:T(8,128)(2,1)S(1)}, u32[]{:S(2)}, u32[]{:S(2)}) collective-permute-start(bf16[128,768]{1,0:T(8,128)(2,1)S(1)} %get-tuple-element.18), channel_id=1, source_target_pairs={{0,1},{1,2},{2,3},{3,0},{4,5},{5,6},{6,7},{7,4},{8,9},{9,10},{10,1... | collective-permute-start | bytes 589832 | tf_op jit(solution)/shard_map/ppermute | solution.py:26
  160.5 16.2 %collective-permute-start.27 = (bf16[128,768]{1,0:T(8,128)(2,1)S(1)}, bf16[128,768]{1,0:T(8,128)(2,1)S(1)}, u32[]{:S(2)}, u32[]{:S(2)}) collective-permute-start(bf16[128,768]{1,0:T(8,128)(2,1)S(1)} %get-tuple-element.20), channel_id=1, source_target_pairs={{0,3},{1,0},{2,1},{3,2},{4,7},{5,4},{6,5},{7,6},{8,11},{9,8},{10,9... | collective-permute-start | bytes 589832 | tf_op jit(solution)/shard_map/ppermute | solution.py:26
  163.5 13.3 %collective-permute-start.28 = (bf16[128,768]{1,0:T(8,128)(2,1)S(1)}, bf16[128,768]{1,0:T(8,128)(2,1)S(1)}, u32[]{:S(2)}, u32[]{:S(2)}) collective-permute-start(bf16[128,768]{1,0:T(8,128)(2,1)S(1)} %get-tuple-element.19), channel_id=1, source_target_pairs={{0,2},{1,3},{2,0},{3,1},{4,6},{5,7},{6,4},{7,5},{8,10},{9,11},{10,... | collective-permute-start | bytes 589832 | tf_op jit(solution)/shard_map/ppermute | solution.py:26
  168.9 12.2 %collective-permute-start.31 = (bf16[128,768]{1,0:T(8,128)(2,1)S(1)}, bf16[128,768]{1,0:T(8,128)(2,1)S(1)}, u32[]{:S(2)}, u32[]{:S(2)}) collective-permute-start(bf16[128,768]{1,0:T(8,128)(2,1)S(1)} %get-tuple-element.21), channel_id=1, source_target_pairs={{0,1},{1,2},{2,3},{3,0},{4,5},{5,6},{6,7},{7,4},{8,9},{9,10},{10,1... | collective-permute-start | bytes 589832 | tf_op jit(solution)/shard_map/ppermute | solution.py:26
  168.9 16.1 %collective-permute-start.32 = (bf16[128,768]{1,0:T(8,128)(2,1)S(1)}, bf16[128,768]{1,0:T(8,128)(2,1)S(1)}, u32[]{:S(2)}, u32[]{:S(2)}) collective-permute-start(bf16[128,768]{1,0:T(8,128)(2,1)S(1)} %get-tuple-element.23), channel_id=1, source_target_pairs={{0,3},{1,0},{2,1},{3,2},{4,7},{5,4},{6,5},{7,6},{8,11},{9,8},{10,9... | collective-permute-start | bytes 589832 | tf_op jit(solution)/shard_map/ppermute | solution.py:26
  175.2 10.2 %collective-permute-start.33 = (bf16[128,768]{1,0:T(8,128)(2,1)S(1)}, bf16[128,768]{1,0:T(8,128)(2,1)S(1)}, u32[]{:S(2)}, u32[]{:S(2)}) collective-permute-start(bf16[128,768]{1,0:T(8,128)(2,1)S(1)} %get-tuple-element.22), channel_id=1, source_target_pairs={{0,2},{1,3},{2,0},{3,1},{4,6},{5,7},{6,4},{7,5},{8,10},{9,11},{10,... | collective-permute-start | bytes 589832 | tf_op jit(solution)/shard_map/ppermute | solution.py:26
  176.7 11.2 %collective-permute-start.36 = (bf16[128,768]{1,0:T(8,128)(2,1)S(1)}, bf16[128,768]{1,0:T(8,128)(2,1)S(1)}, u32[]{:S(2)}, u32[]{:S(2)}) collective-permute-start(bf16[128,768]{1,0:T(8,128)(2,1)S(1)} %get-tuple-element.24), channel_id=1, source_target_pairs={{0,1},{1,2},{2,3},{3,0},{4,5},{5,6},{6,7},{7,4},{8,9},{9,10},{10,1... | collective-permute-start | bytes 589832 | tf_op jit(solution)/shard_map/ppermute | solution.py:26
  176.9 12.0 %collective-permute-start.37 = (bf16[128,768]{1,0:T(8,128)(2,1)S(1)}, bf16[128,768]{1,0:T(8,128)(2,1)S(1)}, u32[]{:S(2)}, u32[]{:S(2)}) collective-permute-start(bf16[128,768]{1,0:T(8,128)(2,1)S(1)} %get-tuple-element.26), channel_id=1, source_target_pairs={{0,3},{1,0},{2,1},{3,2},{4,7},{5,4},{6,5},{7,6},{8,11},{9,8},{10,9... | collective-permute-start | bytes 589832 | tf_op jit(solution)/shard_map/ppermute | solution.py:26
  181.2 11.7 %collective-permute-start.38 = (bf16[128,768]{1,0:T(8,128)(2,1)S(1)}, bf16[128,768]{1,0:T(8,128)(2,1)S(1)}, u32[]{:S(2)}, u32[]{:S(2)}) collective-permute-start(bf16[128,768]{1,0:T(8,128)(2,1)S(1)} %get-tuple-element.25), channel_id=1, source_target_pairs={{0,2},{1,3},{2,0},{3,1},{4,6},{5,7},{6,4},{7,5},{8,10},{9,11},{10,... | collective-permute-start | bytes 589832 | tf_op jit(solution)/shard_map/ppermute | solution.py:26
  195.2 2.7 %copy-start.1 = (bf16[512,3072]{1,0:T(8,128)(2,1)S(1)}, bf16[512,3072]{1,0:T(8,128)(2,1)}, u32[]{:S(2)}) copy-start(bf16[512,3072]{1,0:T(8,128)(2,1)} %param.6) | copy-start | bytes 9437188
  (11 other events, 18.5 us)
Sparse Core Ops, SparseCore 0:
  17.0 41.2 all-gather.1
